TPU v7x, 32 devices: a whole 2x2x4 slice. The times are simulated.
32 devices in a mesh: grp: 2 (over y), region: 4 (over z), batch: 2 (over x), sub: 2 (over core).
Axes of the slice: x: 2, y: 2, z: 4, core: 2. Of those that a mesh axis runs over, the one named last changes fastest.
Arguments:
- params: float32 [8, 640, 128], P(('grp', 'region')), parts along dimension 0
- first_moment: float32 [8, 640, 128], P(('grp', 'region'), ('batch', 'sub')), parts along dimension 0, may hold values from -0.0006 to 0.0006
- second_moment: float32 [8, 640, 128], P(('grp', 'region'), ('batch', 'sub')), parts along dimension 0, may hold values from 1e-09 to 1e-07
- points: float32 [2, 4, 3, 32, 2048], P(None, 'region', None, None, ('grp', 'batch', 'sub')), parts along dimension 4, may hold values from -1 to 1
- deltas: float32 [2, 4, 32, 2048], P(None, 'region', None, ('grp', 'batch', 'sub')), parts along dimension 3, may hold values from 0.03125 to 0.25
- counts: int32 [2, 4, 2048], P(None, 'region', ('grp', 'batch', 'sub')), parts along dimension 2, may hold values from 0 to 32, as said below
- order: int32 [2, 2048, 4], P(None, ('grp', 'batch', 'sub')), parts along dimension 1, may hold values from 0 to 3, each once within a row
- targets: float32 [2, 3, 2048], P(None, None, ('grp', 'batch', 'sub')), parts along dimension 2, may hold values from 0 to 1
Outputs:
- new_params: float32 [8, 640, 128], P(('grp', 'region')), parts along dimension 0
- new_first: float32 [8, 640, 128], P(('grp', 'region'), ('batch', 'sub')), parts along dimension 0
- new_second: float32 [8, 640, 128], P(('grp', 'region'), ('batch', 'sub')), parts along dimension 0
There are 2 independent parts, one for each index of `grp`. A program takes and returns all parts, laid end to end along the dimension named above; each array names one. Nothing has to cross between parts.
Inputs may be any that keep to these rules, and one draw needn't show every extreme that they name: `counts`: every region holds a ray with 32 samples in every step.
All inputs are finite; a program needn't handle non-finite values.
Results may differ from a plain program's by a relative error of at most 0.015.
The roundings to bfloat16 on the way count: a program that leaves them out, or rounds other values in their place, can miss the bound.
Values sent between devices are 32-bit elements; how exact they have to be, the bound alone decides.
A program may use at most 64 MiB of HBM per device.

v0:
```python
import math

import jax
import jax.numpy as jnp
from jax import lax
from jax.sharding import PartitionSpec as P

WIDTH = 256
FREQS = 10
STEPS = 2


BETA_ONE = 0.9
BETA_TWO = 0.999
LEARNING_RATE = 0.02
ADAM_EPSILON = 1e-08


def unpack(weights_flat):
    flattened = weights_flat.reshape(-1)
    first_end = 6 * FREQS * WIDTH
    second_end = first_end + WIDTH * WIDTH
    w_first = flattened[:first_end].reshape(6 * FREQS, WIDTH).astype(jnp.bfloat16)
    w_second = flattened[first_end:second_end].reshape(WIDTH, WIDTH).astype(jnp.bfloat16)
    w_third = flattened[second_end:].reshape(WIDTH, 4).astype(jnp.bfloat16)
    return (w_first, w_second, w_third)


def radiance(weights_flat, sample_points, spacing, live_count):
    samples, ray_count = spacing.shape
    sample_total = samples * ray_count
    frequency = 2.0 ** jnp.arange(FREQS).astype(jnp.float32) * math.pi
    phases = (sample_points[:, None, :, :] * frequency[None, :, None, None]).reshape(
        3 * FREQS, sample_total
    )
    encoded = jnp.concatenate([jnp.sin(phases), jnp.cos(phases)], 0).astype(jnp.bfloat16)
    w_first, w_second, w_third = unpack(weights_flat)
    first_act = jax.nn.relu(jnp.dot(w_first.T, encoded, preferred_element_type=jnp.float32)).astype(
        jnp.bfloat16
    )
    second_act = jax.nn.relu(
        jnp.dot(w_second.T, first_act, preferred_element_type=jnp.float32)
    ).astype(jnp.bfloat16)
    network_out = jnp.dot(w_third.T, second_act, preferred_element_type=jnp.float32)
    density = jax.nn.softplus(network_out[0]).reshape(samples, ray_count)
    colour = jax.nn.sigmoid(network_out[1:]).reshape(3, samples, ray_count)
    inside = (
        lax.broadcasted_iota(jnp.int32, (samples, ray_count), 0) < live_count[None, :]
    ).astype(jnp.float32)
    optical_depth = density * spacing * inside
    depth_sum = jnp.sum(optical_depth, 0)
    prior_depth = jnp.cumsum(optical_depth, 0) - optical_depth
    sample_weight = jnp.exp(-prior_depth) * (1.0 - jnp.exp(-optical_depth))
    shaded_colour = jnp.sum(sample_weight[None] * colour, 1)
    return (depth_sum, shaded_colour)


def coefficients(depth_sums, colours, depth_ranks, target, rays_total):
    earlier = (depth_ranks[None, :, :] < depth_ranks[:, None, :]).astype(jnp.float32)
    prior_depth = jnp.sum(earlier * depth_sums[None, :, :], 1)
    passing = jnp.exp(-prior_depth)
    lighted = passing[:, None, :] * colours
    rendered = jnp.sum(lighted, 0)
    pixel_error = 2.0 * (rendered - target) / rays_total
    behind = (depth_ranks[None, :, :] > depth_ranks[:, None, :]).astype(jnp.float32)
    light_after = jnp.sum(behind[:, :, None, :] * lighted[None], 1)
    d_depth = -jnp.sum(light_after * pixel_error[None], 1)
    d_colour = passing[:, None, :] * pixel_error[None]
    return (d_depth, d_colour)


def body(params, first_moment, second_moment, points, deltas, counts, order, targets):
    groups = lax.axis_size(("batch", "sub"))
    region_index = lax.axis_index("region")
    group_index = lax.axis_index(("batch", "sub"))
    rays_dev = targets.shape[2]
    rays_total = float(rays_dev * groups)
    weights_flat = params[0]
    moment_one = first_moment[0]
    moment_two = second_moment[0]
    shard_rows = moment_one.shape[0]
    for iteration in range(STEPS):
        sample_points = points[iteration, 0]
        spacing = deltas[iteration, 0]
        live_count = counts[iteration, 0]

        def local_field(weights_in):
            return radiance(weights_in, sample_points, spacing, live_count)

        (depth_sum, shaded_colour), pullback = jax.vjp(local_field, weights_flat)
        summary = jnp.concatenate([depth_sum[None], shaded_colour], 0)[None]
        depth_ranks = order[iteration].T
        gathered = lax.all_gather(summary, "region", axis=0, tiled=True)
        d_depth, d_colour = coefficients(
            gathered[:, 0], gathered[:, 1:], depth_ranks, targets[iteration], rays_total
        )
        own_depth = lax.dynamic_index_in_dim(d_depth, region_index, 0, keepdims=False)
        own_colour = lax.dynamic_index_in_dim(d_colour, region_index, 0, keepdims=False)
        gradient = pullback((own_depth, own_colour))[0]
        summed = lax.psum(gradient, ("batch", "sub"))
        gradient_part = lax.dynamic_slice_in_dim(summed, group_index * shard_rows, shard_rows, 0)
        current = lax.dynamic_slice_in_dim(weights_flat, group_index * shard_rows, shard_rows, 0)
        moment_one = BETA_ONE * moment_one + (1.0 - BETA_ONE) * gradient_part
        moment_two = BETA_TWO * moment_two + (1.0 - BETA_TWO) * gradient_part * gradient_part
        updated = current - LEARNING_RATE * moment_one / (jnp.sqrt(moment_two) + ADAM_EPSILON)
        weights_flat = lax.all_gather(updated, ("batch", "sub"), axis=0, tiled=True)
    return (weights_flat[None], moment_one[None], moment_two[None])


def solution(mesh):
    placed = (
        P(("grp", "region"), None, None),
        P(("grp", "region"), ("batch", "sub"), None),
        P(("grp", "region"), ("batch", "sub"), None),
        P(None, "region", None, None, ("grp", "batch", "sub")),
        P(None, "region", None, ("grp", "batch", "sub")),
        P(None, "region", ("grp", "batch", "sub")),
        P(None, ("grp", "batch", "sub"), None),
        P(None, None, ("grp", "batch", "sub")),
    )
    return jax.shard_map(
        body,
        mesh=mesh,
        in_specs=placed,
        out_specs=(
            P(("grp", "region"), None, None),
            P(("grp", "region"), ("batch", "sub"), None),
            P(("grp", "region"), ("batch", "sub"), None),
        ),
        check_vma=False,
    )
```

profile of v0, /device:TPU:0, one launch (start us, length us, event | category | flops | bytes accessed | tf_op | source)
XLA Modules:
  0.0 204.4 jit_solution(12177914756421996232)
XLA Ops:
  7.2 1.0 convert.42
  8.3 0.2 convert_element_type.131
  8.5 1.0 slice_bitcast_fusion
  9.6 0.1 pad.73
  9.7 0.6 copy.37
  10.5 0.1 pad.72
  10.6 0.6 copy.29
  11.3 8.0 %sine_convert_fusion = (bf16[30,8192]{1,0:T(8,128)(2,1)S(1)}, bf16[30,8192]{1,0:T(8,128)(2,1)S(1)}, bf16[30,8192]{1,0:T(8,128)(2,1)S(1)}, bf16[30,8192]{1,0:T(8,128)(2,1)S(1)}) fusion(f32[30,8192]{1,0:T(8,128)S(1)} %bitcast.151, f32[30]{0:T(128)S(1)} %mul.385, f32[30,8192]{1,0:T(8,128)S(1)} %bitcast.152), kind=kLoop, calls=%fused_computation.37 | loop fusion | flops 1474560 | bytes 3932280 | tf_op jit(solution)/shard_map/convert.19
  19.3 1.3 fusion.26
  20.6 1.2 fusion.11
  21.8 2.0 copy-done
  23.8 1.2 convolution_bitcast_fusion
  25.0 2.0 copy-done.1
  27.4 15.0 %all-gather.2 = f32[4,4,256]{2,1,0:T(4,128)S(1)} all-gather(f32[1,4,256]{2,1,0:T(4,128)S(1)} %maximum_bitcast_fusion), channel_id=2, replica_groups=mesh['grp'=2,'region'=4,'batch'=2,'sub'=2] {'region'}, dimensions={0}, use_global_device_ids=true | all-gather | bytes 20480 | tf_op jit(solution)/shard_map/all_gather | solution.py:93
  42.9 0.2 fusion.27
  43.1 0.2 reduce_window_sum.44
  43.4 6.7 %fusion.7 = bf16[8192,256]{1,0:T(8,128)(2,1)} fusion(bf16[256,4]{1,0:T(8,128)(2,1)S(1)} %convert_element_type.131, f32[8192,256]{1,0:T(8,128)} %copy-done.1, f32[1,8192]{1,0:T(1,128)S(1)} %bitcast.172, f32[3,8192]{1,0:T(4,128)S(1)} %get-tuple-element.28), kind=kOutput, calls=%fused_computation.11 | convolution fusion | flops 25198592 | bytes 12716032 | tf_op jit(solution)/shard_map/transpose(jvp())/dot_general | solution.py:44
  50.0 7.0 %fusion.22 = bf16[60,256]{1,0:T(8,128)(2,1)S(1)} fusion(bf16[8192,256]{1,0:T(8,128)(2,1)} %fusion.7, bf16[256,256]{1,0:T(8,128)(2,1)S(1)} %convert_element_type.129, f32[8192,256]{1,0:T(8,128)} %copy-done, bf16[30,8192]{1,0:T(8,128)(2,1)S(1)} %get-tuple-element.40, bf16[30,8192]{1,0:T(8,128)(2,1)S(1)} %get-tuple-element.41), kind=kOutput, calls=%fused_computation.31 | convolution fusion | flops 1333657600 | bytes 13727744 | tf_op jit(solution)/shard_map/transpose(jvp())/dot_general | solution.py:38
  57.0 5.9 %fusion.19 = bf16[32,2,8,128]{3,2,1,0:T(8,128)(2,1)S(1)} fusion(bf16[8192,256]{1,0:T(8,128)(2,1)} %fusion.7, f32[8192,256]{1,0:T(8,128)} %copy-done), kind=kOutput, calls=%fused_computation.28 | convolution fusion | flops 1077936128 | bytes 12713984 | tf_op jit(solution)/shard_map/transpose(jvp())/dot_general | solution.py:42
  62.9 4.1 %fusion.24 = bf16[256,4]{0,1:T(4,128)(2,1)S(1)} fusion(f32[8192,256]{1,0:T(8,128)} %copy-done.1, f32[1,8192]{1,0:T(1,128)S(1)} %bitcast.173, f32[3,8192]{1,0:T(4,128)S(1)} %get-tuple-element.28), kind=kOutput, calls=%fused_computation.33 | convolution fusion | flops 21005312 | bytes 8521728 | tf_op jit(solution)/shard_map/transpose(jvp())/dot_general | solution.py:44
  67.0 0.1 copy.36
  67.1 0.1 copy.21
  67.3 0.1 reshape.248
  67.4 0.8 add_bitcast_fusion.1
  68.3 33.4 %all-reduce.13.cloned.1.call-done = f32[640,128]{1,0:T(8,128)} async-done(((f32[640,128]{1,0:T(8,128)}), f32[640,128]{1,0:T(8,128)}) %all-reduce.13.cloned.1.call-update) | async-done | bytes 327696 | tf_op jit(solution)/shard_map/psum | solution.py:100
  101.8 1.0 bitcast_subtract_fusion
  102.7 6.0 %all_gather.13 = f32[640,128]{1,0:T(8,128)S(1)} all-gather(f32[160,128]{1,0:T(8,128)S(1)} %bitcast_subtract_fusion), channel_id=1, replica_groups=mesh['grp'=2,'region'=4,'batch'=2,'sub'=2] {'batch','sub'}, dimensions={0}, use_global_device_ids=true | all-gather | bytes 409600 | tf_op jit(solution)/shard_map/all_gather | solution.py:106
  108.8 0.2 convert_element_type.144
  109.0 1.3 fusion.25
  110.3 1.3 fusion.14
  111.6 1.9 copy-done.3
  113.5 0.7 fusion.16
  114.2 2.5 %copy-done.2 = f32[256,8192]{1,0:T(8,128)} copy-done((f32[256,8192]{1,0:T(8,128)}, f32[256,8192]{1,0:T(8,128)S(1)}, u32[]{:S(2)}) %copy-start.2) | copy-done | bytes 8388632
  117.0 13.4 %all-gather.3 = f32[4,4,256]{2,1,0:T(4,128)S(1)} all-gather(f32[1,4,256]{2,1,0:T(4,128)S(1)} %maximum_bitcast_fusion.1), channel_id=3, replica_groups=mesh['grp'=2,'region'=4,'batch'=2,'sub'=2] {'region'}, dimensions={0}, use_global_device_ids=true | all-gather | bytes 20480 | tf_op jit(solution)/shard_map/all_gather | solution.py:93
  130.8 0.2 fusion.28
  131.1 0.2 reduce_window_sum.48
  131.3 6.5 %fusion.3 = bf16[256,8192]{1,0:T(8,128)(2,1)} fusion(bf16[256,4]{1,0:T(8,128)(2,1)S(1)} %convert_element_type.144, f32[256,8192]{1,0:T(8,128)} %copy-done.2, f32[1,8192]{1,0:T(1,128)S(1)} %bitcast.174, f32[3,8192]{1,0:T(4,128)S(1)} %get-tuple-element.26), kind=kOutput, calls=%fused_computation.5 | convolution fusion | flops 25198592 | bytes 12716032 | tf_op jit(solution)/shard_map/transpose(jvp())/dot_general | solution.py:44
  137.9 7.2 %fusion.21 = bf16[60,256]{1,0:T(8,128)(2,1)S(1)} fusion(bf16[256,256]{1,0:T(8,128)(2,1)S(1)} %convert_element_type.140, bf16[256,8192]{1,0:T(8,128)(2,1)} %fusion.3, f32[256,8192]{1,0:T(8,128)} %copy-done.3, bf16[30,8192]{1,0:T(8,128)(2,1)S(1)} %get-tuple-element.20, bf16[30,8192]{1,0:T(8,128)(2,1)S(1)} %get-tuple-element.19), kind=kOutput, calls=%fused_computation.30 | convolution fusion | flops 1333657600 | bytes 13727744 | tf_op jit(solution)/shard_map/transpose(jvp())/dot_general | solution.py:38
  145.1 5.9 %fusion.20 = bf16[32,2,8,128]{3,2,1,0:T(8,128)(2,1)S(1)} fusion(bf16[256,8192]{1,0:T(8,128)(2,1)} %fusion.3, f32[256,8192]{1,0:T(8,128)} %copy-done.3), kind=kOutput, calls=%fused_computation.29 | convolution fusion | flops 1077936128 | bytes 12713984 | tf_op jit(solution)/shard_map/transpose(jvp())/dot_general | solution.py:42
  150.9 4.6 %fusion.23 = bf16[256,4]{0,1:T(4,128)(2,1)S(1)} fusion(f32[256,8192]{1,0:T(8,128)} %copy-done.2, f32[1,8192]{1,0:T(1,128)S(1)} %bitcast.175, f32[3,8192]{1,0:T(4,128)S(1)} %get-tuple-element.26), kind=kOutput, calls=%fused_computation.32 | convolution fusion | flops 21005312 | bytes 8521728 | tf_op jit(solution)/shard_map/transpose(jvp())/dot_general | solution.py:44
  155.5 0.1 copy.44
  155.6 0.1 copy.24
  155.8 0.1 reshape.254
  155.9 0.8 add_bitcast_fusion
  156.7 32.6 %all-reduce.15.cloned.1.call-done = f32[640,128]{1,0:T(8,128)} async-done(((f32[640,128]{1,0:T(8,128)}), f32[640,128]{1,0:T(8,128)}) %all-reduce.15.cloned.1.call-update) | async-done | bytes 327696 | tf_op jit(solution)/shard_map/psum | solution.py:100
  189.3 1.7 fusion.72
  190.9 6.0 %all_gather.15 = f32[640,128]{1,0:T(8,128)S(1)} all-gather(f32[160,128]{1,0:T(8,128)S(1)} %get-tuple-element.24), channel_id=1, replica_groups=mesh['grp'=2,'region'=4,'batch'=2,'sub'=2] {'batch','sub'}, dimensions={0}, use_global_device_ids=true | all-gather | bytes 409600 | tf_op jit(solution)/shard_map/all_gather | solution.py:106
  196.9 0.7 copy.64
  (111 shorter events, 2.2 us)
Async XLA Ops:
  7.2 94.6 %all-reduce.13.cloned.1.call-start = ((), (), s32[]{:S(2)}) async-start(), calls=%async_computation | async-start | bytes 655360 | tf_op jit(solution)/shard_map/psum | solution.py:100
  20.6 3.2 %copy-start = (f32[8192,256]{1,0:T(8,128)}, f32[8192,256]{1,0:T(8,128)S(1)}, u32[]{:S(2)}) copy-start(f32[8192,256]{1,0:T(8,128)S(1)} %fusion.26) | copy-start | bytes 25165828
  23.8 3.2 %copy-start.1 = (f32[8192,256]{1,0:T(8,128)}, f32[8192,256]{1,0:T(8,128)S(1)}, u32[]{:S(2)}) copy-start(f32[8192,256]{1,0:T(8,128)S(1)} %fusion.11) | copy-start | bytes 25165828
  23.8 3.3 %copy-start.6 = (f32[2,1,32,256]{3,2,1,0:T(8,128)S(1)}, f32[2,1,32,256]{3,2,1,0:T(8,128)}, u32[]{:S(2)}) copy-start(f32[2,1,32,256]{3,2,1,0:T(8,128)} %param.13) | copy-start | bytes 196612
  23.8 3.4 %copy-start.9 = (s32[2,1,256]{2,1,0:T(1,128)S(1)}, s32[2,1,256]{2,1,0:T(1,128)}, u32[]{:S(2)}) copy-start(s32[2,1,256]{2,1,0:T(1,128)} %param.14) | copy-start | bytes 6148
  23.8 18.6 %copy-start.7 = (s32[2,256,4]{1,2,0:T(4,128)S(1)}, s32[2,256,4]{1,2,0:T(4,128)}, u32[]{:S(2)}) copy-start(s32[2,256,4]{1,2,0:T(4,128)} %param.15) | copy-start | bytes 24580
  23.8 18.7 %copy-start.8 = (f32[2,3,256]{2,0,1:T(2,128)S(1)}, f32[2,3,256]{2,0,1:T(2,128)}, u32[]{:S(2)}) copy-start(f32[2,3,256]{2,0,1:T(2,128)} %param.16) | copy-start | bytes 18436
  62.9 38.8 %copy-start.4 = (f32[1,160,128]{2,1,0:T(8,128)S(1)}, f32[1,160,128]{2,1,0:T(8,128)}, u32[]{:S(2)}) copy-start(f32[1,160,128]{2,1,0:T(8,128)} %param.10) | copy-start | bytes 245764
  62.9 38.8 %copy-start.5 = (f32[1,160,128]{2,1,0:T(8,128)S(1)}, f32[1,160,128]{2,1,0:T(8,128)}, u32[]{:S(2)}) copy-start(f32[1,160,128]{2,1,0:T(8,128)} %param.11) | copy-start | bytes 245764
  68.2 121.1 %all-reduce.15.cloned.1.call-start = ((), (), s32[]{:S(2)}) async-start(), calls=%async_computation.1 | async-start | bytes 655360 | tf_op jit(solution)/shard_map/psum | solution.py:100
  110.3 3.2 %copy-start.3 = (f32[256,8192]{1,0:T(8,128)}, f32[256,8192]{1,0:T(8,128)S(1)}, u32[]{:S(2)}) copy-start(f32[256,8192]{1,0:T(8,128)S(1)} %fusion.25) | copy-start | bytes 25165828
  113.5 3.2 %copy-start.2 = (f32[256,8192]{1,0:T(8,128)}, f32[256,8192]{1,0:T(8,128)S(1)}, u32[]{:S(2)}) copy-start(f32[256,8192]{1,0:T(8,128)S(1)} %fusion.14) | copy-start | bytes 25165828
Sparse Core Ops, SparseCore 0:
  68.3 33.3 all-reduce.12
  156.8 32.3 all-reduce.14
where the time goes:
time: 205 us; the launch traced here: 204 us
  waiting for transfers between devices  66 us (32%)
  matrix products  54.8 us (27%)
  blocking collectives  40.3 us (20%)
  other arithmetic  14.9 us (7%)
  between operations  14.8 us (7%)
  local copies, waits for them, and re-layouts  13.6 us (7%)
    psum x2, waiting for transfers between devices, body(): summed = lax.psum(gradient, ('batch', 'sub'))  66 us
    all_gather x2, blocking collectives, body(): gathered = lax.all_gather(summary, 'region', axis=0, tiled=True)  28.4 us
    dot_general x6, matrix products, radiance(): jnp.dot(w_third.T, second_act, preferred_element_type=jnp.float32)  23.7 us
    dot_general x4, matrix products, radiance(): jnp.dot(w_first.T, encoded, preferred_element_type=jnp.float32)  16.8 us
    dot_general x4, matrix products, radiance(): jnp.dot(w_second.T, first_act, preferred_element_type=jnp.float32)  14.3 us
    all_gather x2, blocking collectives, body(): weights_flat = lax.all_gather(updated, ('batch', 'sub'), axis=0, tiled=True)  11.9 us
    unnamed x44, local copies, waits for them, and re-layouts  11.2 us
    another operation x3, other arithmetic  9 us
  transfers between devices with their start and end apart: 2, of which 2 were waited for; matrix products, arithmetic and copies ran while one was open for 0% of the time, Pallas kernels for 0%

commit v1 on v0

v1 whole, which is shorter than its diff:
```python
import functools
import math

import jax
import jax.numpy as jnp
from jax import lax
from jax.experimental import pallas as pl
from jax.experimental.pallas import tpu as pltpu
from jax.sharding import PartitionSpec as P

WIDTH = 256
FREQS = 10
HALF = FREQS // 2

BETA_ONE = 0.9
BETA_TWO = 0.999
LEARNING_RATE = 0.02
ADAM_EPSILON = 1e-08

HIGH = lax.Precision.HIGHEST
F32 = jnp.float32
BF16 = jnp.bfloat16
MESH = pl.DeviceIdType.MESH
SLOTS = 4
FIRST = 12 * FREQS
SECOND = FIRST + 2 * WIDTH


def dot(a, b, precision=None):
    return lax.dot_general(
        a, b, (((1,), (0,)), ((), ())), precision=precision, preferred_element_type=F32
    )


def dot_nt(a, b, precision=None):
    return lax.dot_general(
        a, b, (((1,), (1,)), ((), ())), precision=precision, preferred_element_type=F32
    )


def iota(shape, dim):
    return lax.broadcasted_iota(jnp.int32, shape, dim)


def one(mask):
    return jnp.where(mask, 1.0, 0.0).astype(F32)


def sine_cosine(turns):
    turns = turns - 2.0 * jnp.floor(turns * 0.5 + 0.5)
    y = turns * (math.pi / 2)
    z = y * y
    s = -1.0 / 39916800.0
    for coefficient in (1.0 / 362880.0, -1.0 / 5040.0, 1.0 / 120.0, -1.0 / 6.0, 1.0):
        s = s * z + coefficient
    s = s * y
    c = 1.0 / 479001600.0
    for coefficient in (
        -1.0 / 3628800.0,
        1.0 / 40320.0,
        -1.0 / 720.0,
        1.0 / 24.0,
        -0.5,
        1.0,
    ):
        c = c * z + coefficient
    return doubled(s, c)


def doubled(s, c):
    s2 = s + s
    return s2 * c, 1.0 - s2 * s


def kernel(
    steps,
    regions,
    batches,
    subs,
    params_ref,
    first_ref,
    second_ref,
    points_ref,
    deltas_ref,
    counts_ref,
    order_ref,
    targets_ref,
    out_params,
    out_first,
    out_second,
    enc_s,
    h1_s,
    h2_s,
    raw_s,
    dout_s,
    w1_s,
    w1t_s,
    w2_s,
    w2t_s,
    w3_s,
    w3t_s,
    g1_s,
    g2_s,
    g3_s,
    grad_s,
    weights_s,
    gath_s,
    part_s,
    gsend,
    grecv,
    rsend,
    rrecv,
    asend,
    arecv,
):
    samples, rays = deltas_ref.shape[2], deltas_ref.shape[3]
    groups = batches * subs
    shard = first_ref.shape[1]
    rays_total = float(rays * groups)
    region = lax.axis_index("region")
    group = lax.axis_index("batch") * subs + lax.axis_index("sub")
    columns = SLOTS * rays
    chunks = samples // SLOTS
    tiles = rays // 128

    def group_peer(offset):
        peer = lax.rem(group + offset, groups)
        return peer, {"batch": lax.div(peer, subs), "sub": lax.rem(peer, subs)}

    def region_peer(offset):
        return {"region": lax.rem(region + offset, regions)}

    barrier = pltpu.get_barrier_semaphore()
    for offset in range(1, regions):
        pl.semaphore_signal(barrier, inc=1, device_id=region_peer(offset), device_id_type=MESH)
    for offset in range(1, groups):
        pl.semaphore_signal(
            barrier, inc=1, device_id=group_peer(offset)[1], device_id_type=MESH
        )

    dout_s[...] = jnp.zeros_like(dout_s)
    hidden = iota((WIDTH, 128), 0)
    lane = iota((WIDTH, 128), 1)
    third_mask = (lane >> 2) == (hidden & 31)
    spread = one((iota((WIDTH, 8), 0) >> 5) == iota((WIDTH, 8), 1))
    spread_t = one((iota((8, WIDTH), 1) >> 5) == iota((8, WIDTH), 0))
    pick = one((iota((128, 16), 0) & 3) == iota((128, 16), 1))
    pick_t = one((iota((16, 128), 1) & 3) == iota((16, 128), 0))
    eye = one(iota((WIDTH, WIDTH), 0) == iota((WIDTH, WIDTH), 1))
    eye_half = eye.astype(BF16)
    later = one(iota((samples, samples), 0) < iota((samples, samples), 1))
    earlier = one(iota((samples, samples), 0) > iota((samples, samples), 1))

    for step in range(steps):

        def rows_of(start, size, stride):
            if step == 0:
                return params_ref[0, pl.ds(start, size, stride=stride), :]
            return weights_s[step - 1, pl.ds(start, size, stride=stride), :]

        keep = iota((8, 128), 0) < 6
        for kind in range(2):
            for j in range(HALF):
                at = 8 * (kind * HALF + j)
                for side in range(2):
                    block = rows_of(2 * (kind * 3 * FREQS + j) + side, 8, FREQS)
                    w1_s[at : at + 8, side * 128 : (side + 1) * 128] = jnp.where(
                        keep, block, 0.0
                    )
        for side in range(2):
            w2_s[:, side * 128 : (side + 1) * 128] = rows_of(FIRST + side, WIDTH, 2).astype(BF16)
        w1t_s[...] = dot_nt(eye_half, w1_s[...].astype(BF16)).astype(BF16)
        w2t_s[...] = dot_nt(eye_half, w2_s[...]).astype(BF16)
        third = rows_of(SECOND, 8, 1).astype(BF16).astype(F32)
        wide = jnp.where(third_mask, dot(spread, third, HIGH), 0.0)
        w3_s[...] = dot(wide, pick, HIGH).astype(BF16)
        w3t_s[...] = dot_nt(pick_t, wide, HIGH).astype(BF16)

        row = iota((8, rays), 0)
        scaling = jnp.where((row & 1) == 0, 1.0, float(2**HALF))

        def forward(i, carry):
            column = pl.multiple_of(i * columns, columns)
            for s in range(SLOTS):
                t = i * SLOTS + s
                x, y, z = (
                    jnp.broadcast_to(points_ref[step, 0, c, pl.ds(t, 1), :], (8, rays))
                    for c in range(3)
                )
                where = jnp.where(row < 2, x, jnp.where(row < 4, y, z))
                sine, cosine = sine_cosine(where * scaling)
                sines, cosines = [sine], [cosine]
                for _ in range(HALF - 1):
                    sine, cosine = doubled(sine, cosine)
                    sines.append(sine)
                    cosines.append(cosine)
                enc_s[:, pl.ds(pl.multiple_of(column + s * rays, rays), rays)] = jnp.concatenate(
                    sines + cosines, 0
                ).astype(BF16)
            here = pl.ds(column, columns)
            first = jnp.maximum(dot(w1t_s[...], enc_s[:, here]), 0.0).astype(BF16)
            h1_s[:, here] = first
            second = jnp.maximum(dot(w2t_s[...], first), 0.0).astype(BF16)
            h2_s[:, here] = second
            out = dot(w3t_s[...], second)
            for s in range(SLOTS):
                t = i * SLOTS + s
                for k in range(tiles):
                    at = s * rays + k * 128
                    raw_s[k, pl.ds(pl.multiple_of(t * 8, 8), 8), :] = out[:8, at : at + 128]
            return carry

        lax.fori_loop(0, chunks, forward, 0)

        raw = [
            jnp.concatenate(
                [raw_s[k, pl.ds(c, samples, stride=8), :] for k in range(tiles)], 1
            )
            for c in range(4)
        ]
        spacing = jnp.where(
            iota((samples, rays), 0) < counts_ref[step], deltas_ref[step, 0], 0.0
        )
        density = jnp.maximum(raw[0], 0.0) + jnp.log1p(jnp.exp(-jnp.abs(raw[0])))
        optical = density * spacing
        colour = [jax.nn.sigmoid(value) for value in raw[1:]]
        through = jnp.exp(-dot(earlier, optical, HIGH))
        left = jnp.exp(-optical)
        share = through * (1.0 - left)
        summary = [jnp.sum(optical, 0, keepdims=True)]
        summary += [jnp.sum(share * value, 0, keepdims=True) for value in colour]
        gath_s[step, region] = jnp.concatenate(
            summary + [jnp.zeros((4, rays), F32)], 0
        )

        if step == 0:
            pl.semaphore_wait(barrier, regions - 1 + groups - 1)
        copies = []
        for offset in range(1, regions):
            copy = pltpu.make_async_remote_copy(
                src_ref=gath_s.at[step, region],
                dst_ref=gath_s.at[step, region],
                send_sem=gsend.at[step, offset - 1],
                recv_sem=grecv.at[step, offset - 1],
                device_id=region_peer(offset),
                device_id_type=MESH,
            )
            copy.start()
            copies.append(copy)
        slope = [value * (1.0 - value) * share for value in colour]
        density_slope = jax.nn.sigmoid(raw[0]) * spacing
        ranks = dot_nt(
            one(iota((regions, regions), 0) == iota((regions, regions), 1)),
            order_ref[step].astype(F32),
            HIGH,
        )
        g1_s[...] = jnp.zeros_like(g1_s)
        g2_s[...] = jnp.zeros_like(g2_s)
        g3_s[...] = jnp.zeros_like(g3_s)
        for copy in copies:
            copy.wait()

        depths = [gath_s[step, r, 0:1, :] for r in range(regions)]
        rank = [ranks[r : r + 1] for r in range(regions)]
        rendered = [jnp.zeros((1, rays), F32)] * 3
        lighted, passing_own, rank_own = [], jnp.zeros((1, rays), F32), jnp.zeros((1, rays), F32)
        for r in range(regions):
            prior = jnp.zeros((1, rays), F32)
            for q in range(regions):
                if q != r:
                    prior = prior + jnp.where(rank[q] < rank[r], depths[q], 0.0)
            passing = jnp.exp(-prior)
            lights = [passing * gath_s[step, r, c + 1 : c + 2, :] for c in range(3)]
            lighted.append(lights)
            rendered = [a + b for a, b in zip(rendered, lights)]
            passing_own = jnp.where(region == r, passing, passing_own)
            rank_own = jnp.where(region == r, rank[r], rank_own)
        error = [
            2.0 * (rendered[c] - targets_ref[step, c : c + 1, :]) / rays_total for c in range(3)
        ]
        d_depth = jnp.zeros((1, rays), F32)
        for r in range(regions):
            amount = sum(lighted[r][c] * error[c] for c in range(3))
            d_depth = d_depth - jnp.where(rank[r] > rank_own, amount, 0.0)
        d_colour = [passing_own * value for value in error]

        pull = sum(d_colour[c] * colour[c] for c in range(3))
        after = dot(later, pull * share, HIGH)
        d_optical = pull * through * left - after + d_depth
        d_raw = [d_optical * density_slope] + [d_colour[c] * slope[c] for c in range(3)]
        for c in range(4):
            for k in range(tiles):
                dout_s[k, pl.ds(c, samples, stride=16), :] = d_raw[c][
                    :, k * 128 : (k + 1) * 128
                ]

        def backward(i, carry):
            here = pl.ds(pl.multiple_of(i * columns, columns), columns)
            d_out = jnp.concatenate(
                [
                    dout_s[k, pl.ds(pl.multiple_of((i * SLOTS + s) * 16, 16), 16), :]
                    for s in range(SLOTS)
                    for k in range(tiles)
                ],
                1,
            ).astype(BF16)
            second = h2_s[:, here]
            first = h1_s[:, here]
            zero = jnp.zeros((), BF16)
            g3_s[...] += dot_nt(d_out, second)
            d_second = jnp.where(second > zero, dot(w3_s[...], d_out).astype(BF16), zero)
            d_first = jnp.where(first > zero, dot(w2_s[...], d_second).astype(BF16), zero)
            g2_s[...] += dot_nt(first, d_second)
            g1_s[...] += dot_nt(enc_s[:, here], d_first)
            return carry

        lax.fori_loop(0, chunks, backward, 0)

        for kind in range(2):
            for j in range(HALF):
                at = 8 * (kind * HALF + j)
                for side in range(2):
                    grad_s[
                        step, pl.ds(2 * (kind * 3 * FREQS + j) + side, 6, stride=FREQS), :
                    ] = g1_s[at : at + 6, side * 128 : (side + 1) * 128]
        for side in range(2):
            grad_s[step, pl.ds(FIRST + side, WIDTH, stride=2), :] = g2_s[
                :, side * 128 : (side + 1) * 128
            ]
        third_grad = dot(dot_nt(eye, g3_s[...], HIGH), pick_t, HIGH)
        grad_s[step, SECOND : SECOND + 8, :] = dot(
            spread_t, jnp.where(third_mask, third_grad, 0.0), HIGH
        )

        copies = []
        for offset in range(1, groups):
            peer, where = group_peer(offset)
            copy = pltpu.make_async_remote_copy(
                src_ref=grad_s.at[step, pl.ds(pl.multiple_of(peer * shard, 8), shard), :],
                dst_ref=part_s.at[step, offset - 1],
                send_sem=rsend.at[step, offset - 1],
                recv_sem=rrecv.at[step, offset - 1],
                device_id=where,
                device_id_type=MESH,
            )
            copy.start()
            copies.append(copy)
        mine = pl.ds(pl.multiple_of(group * shard, 8), shard)
        gradient = grad_s[step, mine, :]
        for offset, copy in enumerate(copies):
            copy.wait()
            gradient = gradient + part_s[step, offset]
        if step == 0:
            moment_one, moment_two = first_ref[0], second_ref[0]
            current = params_ref[0, mine, :]
        else:
            moment_one, moment_two = out_first[0], out_second[0]
            current = weights_s[step - 1, mine, :]
        moment_one = BETA_ONE * moment_one + (1.0 - BETA_ONE) * gradient
        moment_two = BETA_TWO * moment_two + (1.0 - BETA_TWO) * gradient * gradient
        out_first[0] = moment_one
        out_second[0] = moment_two
        weights_s[step, mine, :] = current - LEARNING_RATE * moment_one / (
            jnp.sqrt(moment_two) + ADAM_EPSILON
        )
        copies = []
        for offset in range(1, groups):
            copy = pltpu.make_async_remote_copy(
                src_ref=weights_s.at[step, mine, :],
                dst_ref=weights_s.at[step, mine, :],
                send_sem=asend.at[step, offset - 1],
                recv_sem=arecv.at[step, offset - 1],
                device_id=group_peer(offset)[1],
                device_id_type=MESH,
            )
            copy.start()
            copies.append(copy)
        for copy in copies:
            copy.wait()
    out_params[0] = weights_s[steps - 1]


def body(params, first_moment, second_moment, points, deltas, counts, order, targets):
    steps, _, _, samples, rays = points.shape
    regions = lax.axis_size("region")
    batches, subs = lax.axis_size("batch"), lax.axis_size("sub")
    groups = batches * subs
    total = samples * rays
    rows, lanes = params.shape[1:]
    shard = first_moment.shape[1]
    dma = pltpu.SemaphoreType.DMA
    vmem = pl.BlockSpec(memory_space=pltpu.VMEM)
    return pl.pallas_call(
        functools.partial(kernel, steps, regions, batches, subs),
        out_shape=(
            jax.ShapeDtypeStruct(params.shape, F32),
            jax.ShapeDtypeStruct(first_moment.shape, F32),
            jax.ShapeDtypeStruct(second_moment.shape, F32),
        ),
        in_specs=[vmem] * 8,
        out_specs=(vmem,) * 3,
        scratch_shapes=[
            pltpu.VMEM((16 * HALF, total), BF16),
            pltpu.VMEM((WIDTH, total), BF16),
            pltpu.VMEM((WIDTH, total), BF16),
            pltpu.VMEM((rays // 128, samples * 8, 128), F32),
            pltpu.VMEM((rays // 128, samples * 16, 128), F32),
            pltpu.VMEM((16 * HALF, WIDTH), F32),
            pltpu.VMEM((WIDTH, 16 * HALF), BF16),
            pltpu.VMEM((WIDTH, WIDTH), BF16),
            pltpu.VMEM((WIDTH, WIDTH), BF16),
            pltpu.VMEM((WIDTH, 16), BF16),
            pltpu.VMEM((16, WIDTH), BF16),
            pltpu.VMEM((16 * HALF, WIDTH), F32),
            pltpu.VMEM((WIDTH, WIDTH), F32),
            pltpu.VMEM((16, WIDTH), F32),
            pltpu.VMEM((steps, rows, lanes), F32),
            pltpu.VMEM((steps, rows, lanes), F32),
            pltpu.VMEM((steps, regions, 8, rays), F32),
            pltpu.VMEM((steps, groups - 1, shard, lanes), F32),
            dma((steps, regions - 1)),
            dma((steps, regions - 1)),
            dma((steps, groups - 1)),
            dma((steps, groups - 1)),
            dma((steps, groups - 1)),
            dma((steps, groups - 1)),
        ],
        compiler_params=pltpu.CompilerParams(
            collective_id=0, has_side_effects=True, vmem_limit_bytes=48 * 1024 * 1024
        ),
    )(params, first_moment, second_moment, points, deltas, counts, order, targets)


def solution(mesh):
    placed = (
        P(("grp", "region"), None, None),
        P(("grp", "region"), ("batch", "sub"), None),
        P(("grp", "region"), ("batch", "sub"), None),
        P(None, "region", None, None, ("grp", "batch", "sub")),
        P(None, "region", None, ("grp", "batch", "sub")),
        P(None, "region", ("grp", "batch", "sub")),
        P(None, ("grp", "batch", "sub"), None),
        P(None, None, ("grp", "batch", "sub")),
    )
    return jax.shard_map(
        body,
        mesh=mesh,
        in_specs=placed,
        out_specs=(
            P(("grp", "region"), None, None),
            P(("grp", "region"), ("batch", "sub"), None),
            P(("grp", "region"), ("batch", "sub"), None),
        ),
        check_vma=False,
    )
```

time: 205 us -> 64.3 us (0.31)
  waiting for transfers between devices: 66 us -> 0 us
  Pallas kernels: 0 us -> 56.1 us
  matrix products: 54.8 us -> 0 us
  blocking collectives: 40.3 us -> 0 us
  other arithmetic: 14.9 us -> 0 us
  between operations: 14.8 us -> 0.67 us
  local copies, waits for them, and re-layouts: 13.6 us -> 6.34 us
    psum x2 -> x0, waiting for transfers between devices: 66 us -> none  [body(): summed = lax.psum(gradient, ('batch', 'sub'))]
    pallas_call x0 -> x1, Pallas kernels: none -> 56.1 us  [body(): pl.pallas_call(functools.partial(kernel, steps, regions, batches, subs),...]
    dot_general x14 -> x0, matrix products: 54.8 us -> none  [the longest x6 23.7 us: radiance(): jnp.dot(w_third.T, second_act, preferred_element_type=jnp.float32)]
    all_gather x4 -> x0, blocking collectives: 40.3 us -> none  [the longest x2 28.4 us: body(): gathered = lax.all_gather(summary, 'region', axis=0, tiled=True)]
    another operation x7 -> x0, other arithmetic: 9.44 us -> none
    unnamed x44 -> x17, local copies, waits for them, and re-layouts: 11.2 us -> 6.34 us
  transfers between devices with their start and end apart: 2 -> 0, of which waited for: 2 -> 0; matrix products, arithmetic and copies ran while one was open for 0% -> 0% of each run, Pallas kernels for 0% -> 0%
where the time goes in v1:
time: 64.3 us; the launch traced here: 63.1 us
  Pallas kernels  56.1 us (87%)
  local copies, waits for them, and re-layouts  6.34 us (10%)
  between operations  0.67 us (1%)
    pallas_call x1, Pallas kernels, body(): pl.pallas_call(functools.partial(kernel, steps, regions, batches, subs),...  56.1 us
    unnamed x17, local copies, waits for them, and re-layouts  6.34 us

profile of v1, /device:TPU:0, one launch (start us, length us, event | category | flops | bytes accessed | tf_op | source)
XLA Modules:
  0.0 63.1 jit_solution(3224371405580723756)
XLA Ops:
  0.6 0.0 copy-start.1
  0.6 0.7 %copy.12.targets_ref = f32[2,3,256]{2,1,0:T(4,128)S(1)} copy(f32[2,3,256]{2,0,1:T(2,128)} %param.15) | data formatting | bytes 12288 | tf_op args[7]
  1.4 0.0 copy-start.2
  1.4 0.0 copy-start.5
  1.4 0.9 %copy.11.order_ref = s32[2,256,4]{2,1,0:T(8,128)S(1)} copy(s32[2,256,4]{1,2,0:T(4,128)} %param.14) | data formatting | bytes 16384 | tf_op args[6]
  2.3 0.0 copy-done.1
  2.3 0.0 copy-done.2
  2.3 0.0 copy-done.5
  2.3 0.0 copy-start
  2.3 1.0 %copy-done = f32[1,640,128]{2,1,0:T(8,128)S(1)} copy-done((f32[1,640,128]{2,1,0:T(8,128)S(1)}, f32[1,640,128]{2,1,0:T(8,128)}, u32[]{:S(2)}) %copy-start) | copy-done | bytes 327704
  3.3 0.0 copy-start.3
  3.3 0.9 %copy-done.3 = f32[1,160,128]{2,1,0:T(8,128)S(1)} copy-done((f32[1,160,128]{2,1,0:T(8,128)S(1)}, f32[1,160,128]{2,1,0:T(8,128)}, u32[]{:S(2)}) %copy-start.3) | copy-done | bytes 81944
  4.2 0.0 copy-start.4
  4.2 0.8 %copy-done.4 = f32[2,1,32,256]{3,2,1,0:T(8,128)S(1)} copy-done((f32[2,1,32,256]{3,2,1,0:T(8,128)S(1)}, f32[2,1,32,256]{3,2,1,0:T(8,128)}, u32[]{:S(2)}) %copy-start.4) | copy-done | bytes 65560
  5.0 56.1 %shard_map.103 = (f32[1,640,128]{2,1,0:T(8,128)S(1)}, f32[1,160,128]{2,1,0:T(8,128)S(1)}, f32[1,160,128]{2,1,0:T(8,128)S(1)}) custom-call(f32[1,640,128]{2,1,0:T(8,128)S(1)} %copy-done, f32[1,160,128]{2,1,0:T(8,128)S(1)} %copy-done.2, f32[1,160,128]{2,1,0:T(8,128)S(1)} %copy-done.3, f32[2,1,3,32,256]{4,3,2,1,0:T(8,128)S(1)} %copy-done.1, ...), custom_call_target="tpu_custom_call" | custom-call | tf_op jit(solution)/shard_map/pallas_call | solution.py:393
  61.1 0.7 %copy.16 = f32[1,640,128]{2,1,0:T(8,128)} copy(f32[1,640,128]{2,1,0:T(8,128)S(1)} %get-tuple-element.6) | data formatting | bytes 655360
  61.9 0.6 %copy.17 = f32[1,160,128]{2,1,0:T(8,128)} copy(f32[1,160,128]{2,1,0:T(8,128)S(1)} %get-tuple-element.7) | data formatting | bytes 163840
  62.5 0.6 %copy.18 = f32[1,160,128]{2,1,0:T(8,128)} copy(f32[1,160,128]{2,1,0:T(8,128)S(1)} %get-tuple-element.8) | data formatting | bytes 163840
Async XLA Ops:
  0.6 1.6 %copy-start.1 = (f32[2,1,3,32,256]{4,3,2,1,0:T(8,128)S(1)}, f32[2,1,3,32,256]{4,3,2,1,0:T(8,128)}, u32[]{:S(2)}) copy-start(f32[2,1,3,32,256]{4,3,2,1,0:T(8,128)} %points_ref.1) | copy-start | bytes 589828
  1.4 0.9 %copy-start.2 = (f32[1,160,128]{2,1,0:T(8,128)S(1)}, f32[1,160,128]{2,1,0:T(8,128)}, u32[]{:S(2)}) copy-start(f32[1,160,128]{2,1,0:T(8,128)} %first_ref.1) | copy-start | bytes 245764
  1.4 0.9 %copy-start.5 = (s32[2,1,256]{2,1,0:T(1,128)S(1)}, s32[2,1,256]{2,1,0:T(1,128)}, u32[]{:S(2)}) copy-start(s32[2,1,256]{2,1,0:T(1,128)} %counts_ref.1) | copy-start | bytes 6148
  2.3 1.0 %copy-start = (f32[1,640,128]{2,1,0:T(8,128)S(1)}, f32[1,640,128]{2,1,0:T(8,128)}, u32[]{:S(2)}) copy-start(f32[1,640,128]{2,1,0:T(8,128)} %params_ref.1) | copy-start | bytes 983044
  3.3 0.9 %copy-start.3 = (f32[1,160,128]{2,1,0:T(8,128)S(1)}, f32[1,160,128]{2,1,0:T(8,128)}, u32[]{:S(2)}) copy-start(f32[1,160,128]{2,1,0:T(8,128)} %second_ref.1) | copy-start | bytes 245764
  4.2 0.8 %copy-start.4 = (f32[2,1,32,256]{3,2,1,0:T(8,128)S(1)}, f32[2,1,32,256]{3,2,1,0:T(8,128)}, u32[]{:S(2)}) copy-start(f32[2,1,32,256]{3,2,1,0:T(8,128)} %deltas_ref.1) | copy-start | bytes 196612

commit v2 on v1

v2 whole, which is shorter than its diff:
```python
import functools
import math

import jax
import jax.numpy as jnp
from jax import lax
from jax.experimental import pallas as pl
from jax.experimental.pallas import tpu as pltpu
from jax.sharding import PartitionSpec as P

WIDTH = 256
FREQS = 10
HALF = FREQS // 2

BETA_ONE = 0.9
BETA_TWO = 0.999
LEARNING_RATE = 0.02
ADAM_EPSILON = 1e-08

HIGH = lax.Precision.HIGHEST
F32 = jnp.float32
BF16 = jnp.bfloat16
MESH = pl.DeviceIdType.MESH
SLOTS = 32
FIRST = 12 * FREQS
SECOND = FIRST + 2 * WIDTH


def dot(a, b, precision=None):
    return lax.dot_general(
        a, b, (((1,), (0,)), ((), ())), precision=precision, preferred_element_type=F32
    )


def dot_nt(a, b, precision=None):
    return lax.dot_general(
        a, b, (((1,), (1,)), ((), ())), precision=precision, preferred_element_type=F32
    )


def iota(shape, dim):
    return lax.broadcasted_iota(jnp.int32, shape, dim)


def one(mask):
    return jnp.where(mask, 1.0, 0.0).astype(F32)


def sine_cosine(turns):
    turns = turns - 2.0 * jnp.floor(turns * 0.5 + 0.5)
    y = turns * (math.pi / 2)
    z = y * y
    s = -1.0 / 39916800.0
    for coefficient in (1.0 / 362880.0, -1.0 / 5040.0, 1.0 / 120.0, -1.0 / 6.0, 1.0):
        s = s * z + coefficient
    s = s * y
    c = 1.0 / 479001600.0
    for coefficient in (
        -1.0 / 3628800.0,
        1.0 / 40320.0,
        -1.0 / 720.0,
        1.0 / 24.0,
        -0.5,
        1.0,
    ):
        c = c * z + coefficient
    return doubled(s, c)


def doubled(s, c):
    s2 = s + s
    return s2 * c, 1.0 - s2 * s


def kernel(
    steps,
    regions,
    batches,
    subs,
    params_hbm,
    first_hbm,
    second_hbm,
    points_hbm,
    deltas_hbm,
    counts_ref,
    order_ref,
    targets_ref,
    out_params,
    out_first,
    out_second,
    params_ref,
    first_ref,
    second_ref,
    points_ref,
    deltas_ref,
    enc_s,
    h1_s,
    h2_s,
    raw_s,
    dout_s,
    w1_s,
    w1t_s,
    w2_s,
    w2t_s,
    w3_s,
    w3t_s,
    third_s,
    g1_s,
    g2_s,
    g3_s,
    grad_s,
    weights_s,
    gath_s,
    core_s,
    chip_s,
    part_s,
    loads,
    gsend,
    grecv,
    csend,
    crecv,
    rsend,
    rrecv,
    asend,
    arecv,
    bsend,
    brecv,
):
    samples, rays = deltas_ref.shape[2], deltas_ref.shape[3]
    groups = batches * subs
    shard = first_ref.shape[1]
    rays_total = float(rays * groups)
    region = lax.axis_index("region")
    batch = lax.axis_index("batch")
    sub = lax.axis_index("sub")
    columns = SLOTS * 128
    chunks = samples // SLOTS
    parts = rays // 128

    fetches = []
    for k, (source, target) in enumerate(
        (
            (points_hbm, points_ref),
            (params_hbm, params_ref),
            (deltas_hbm, deltas_ref),
            (first_hbm, first_ref),
            (second_hbm, second_ref),
        )
    ):
        fetch = pltpu.make_async_copy(source, target, loads.at[k])
        fetch.start()
        fetches.append(fetch)

    def region_peer(offset):
        return {"region": lax.rem(region + offset, regions)}

    def batch_peer(offset):
        return {"batch": lax.rem(batch + offset, batches)}

    def sub_peer(offset):
        return {"sub": lax.rem(sub + offset, subs)}

    def shard_rows(batch_at, sub_at):
        return pl.ds(pl.multiple_of((batch_at * subs + sub_at) * shard, 8), shard)

    def send(source, target, send_sem, recv_sem, where):
        copy = pltpu.make_async_remote_copy(
            src_ref=source,
            dst_ref=target,
            send_sem=send_sem,
            recv_sem=recv_sem,
            device_id=where,
            device_id_type=MESH,
        )
        copy.start()
        return copy

    barrier = pltpu.get_barrier_semaphore()
    for count, peer in ((regions, region_peer), (batches, batch_peer), (subs, sub_peer)):
        for offset in range(1, count):
            pl.semaphore_signal(
                barrier, inc=1, device_id=peer(offset), device_id_type=MESH
            )

    dout_s[...] = jnp.zeros_like(dout_s)
    flat = iota((4 * WIDTH, 128), 0)
    lane = iota((4 * WIDTH, 128), 1)
    third_s[...] = one(
        ((flat & 31) == (lane >> 2)) & ((flat >> 8) == (lane & 3))
    ).astype(BF16)
    third_mask = ((iota((8, 4 * WIDTH), 1) & (WIDTH - 1)) >> 5) == iota((8, 4 * WIDTH), 0)
    eye_half = one(iota((WIDTH, WIDTH), 0) == iota((WIDTH, WIDTH), 1)).astype(BF16)
    later = one(iota((samples, samples), 0) < iota((samples, samples), 1))
    earlier = one(iota((samples, samples), 0) > iota((samples, samples), 1))
    row = iota((8, 128), 0)
    scaling = jnp.where((row & 1) == 0, 1.0, float(2**HALF))
    keep = row < 6

    def encode(step, part):
        def chunk(i, carry):
            blocks = [
                points_ref[
                    step,
                    0,
                    c,
                    pl.ds(pl.multiple_of(i * SLOTS, SLOTS), SLOTS),
                    part * 128 : (part + 1) * 128,
                ]
                for c in range(3)
            ]
            for s in range(SLOTS):
                t = i * SLOTS + s
                x, y, z = (
                    jnp.broadcast_to(block[s : s + 1], (8, 128)) for block in blocks
                )
                where = jnp.where(row < 2, x, jnp.where(row < 4, y, z))
                sine, cosine = sine_cosine(where * scaling)
                sines, cosines = [sine], [cosine]
                for _ in range(HALF - 1):
                    sine, cosine = doubled(sine, cosine)
                    sines.append(sine)
                    cosines.append(cosine)
                at = pl.multiple_of(part * samples * 128 + t * 128, 128)
                enc_s[step, :, pl.ds(at, 128)] = jnp.concatenate(sines + cosines, 0).astype(
                    BF16
                )
            return carry

        lax.fori_loop(0, chunks, chunk, 0)

    fetches[0].wait()
    for part in range(parts):
        encode(0, part)
    fetches[1].wait()

    for step in range(steps):

        def rows_of(start, size, stride):
            if step == 0:
                return params_ref[0, pl.ds(start, size, stride=stride), :]
            return weights_s[step - 1, pl.ds(start, size, stride=stride), :]

        for kind in range(2):
            for j in range(HALF):
                at = 8 * (kind * HALF + j)
                for side in range(2):
                    block = rows_of(2 * (kind * 3 * FREQS + j) + side, 8, FREQS)
                    w1_s[at : at + 8, side * 128 : (side + 1) * 128] = jnp.where(
                        keep, block, 0.0
                    )
        for side in range(2):
            w2_s[:, side * 128 : (side + 1) * 128] = rows_of(FIRST + side, WIDTH, 2).astype(BF16)
        w1t_s[...] = dot_nt(eye_half, w1_s[...].astype(BF16)).astype(BF16)
        w2t_s[...] = dot_nt(eye_half, w2_s[...]).astype(BF16)
        third = jnp.concatenate([rows_of(SECOND, 8, 1), jnp.zeros((8, 128), F32)], 0)
        wide = dot_nt(third.astype(BF16), third_s[...])[:8]
        wide = jnp.sum(jnp.where(third_mask, wide, 0.0), 0, keepdims=True)
        w3t_s[...] = jnp.concatenate(
            [wide[:, c * WIDTH : (c + 1) * WIDTH] for c in range(4)]
            + [jnp.zeros((12, WIDTH), F32)],
            0,
        ).astype(BF16)
        w3_s[...] = dot_nt(eye_half, w3t_s[...]).astype(BF16)
        g1_s[...] = jnp.zeros_like(g1_s)
        g2_s[...] = jnp.zeros_like(g2_s)
        g3_s[...] = jnp.zeros_like(g3_s)

        kept, exchanges = [], []
        for part in range(parts):
            base = part * samples * 128
            own = slice(part * 128, (part + 1) * 128)

            def forward(i, carry):
                here = pl.ds(pl.multiple_of(base + i * columns, columns), columns)
                first = jnp.maximum(dot(w1t_s[...], enc_s[step, :, here]), 0.0).astype(BF16)
                h1_s[:, here] = first
                second = jnp.maximum(dot(w2t_s[...], first), 0.0).astype(BF16)
                h2_s[:, here] = second
                out = dot(w3t_s[...], second)
                for s in range(SLOTS):
                    raw_s[part, pl.ds(pl.multiple_of((i * SLOTS + s) * 8, 8), 8), :] = out[
                        :8, s * 128 : (s + 1) * 128
                    ]
                return carry

            lax.fori_loop(0, chunks, forward, 0)

            if step == 0 and part == 0:
                fetches[2].wait()
            raw = [raw_s[part, pl.ds(c, samples, stride=8), :] for c in range(4)]
            spacing = jnp.where(
                iota((samples, 128), 0) < counts_ref[step, :, own],
                deltas_ref[step, 0, :, own],
                0.0,
            )
            density = jnp.maximum(raw[0], 0.0) + jnp.log1p(jnp.exp(-jnp.abs(raw[0])))
            optical = density * spacing
            colour = [jax.nn.sigmoid(value) for value in raw[1:]]
            through = jnp.exp(-dot(earlier, optical, HIGH))
            left = jnp.exp(-optical)
            share = through * (1.0 - left)
            summary = [jnp.sum(optical, 0, keepdims=True)]
            summary += [jnp.sum(share * value, 0, keepdims=True) for value in colour]
            gath_s[step, part, region] = jnp.concatenate(
                summary + [jnp.zeros((4, 128), F32)], 0
            )
            if step == 0 and part == 0:
                pl.semaphore_wait(barrier, regions + batches + subs - 3)
            mine = gath_s.at[step, part, region]
            exchanges.append(
                [
                    send(
                        mine,
                        mine,
                        gsend.at[step, part, offset - 1],
                        grecv.at[step, part, offset - 1],
                        region_peer(offset),
                    )
                    for offset in range(1, regions)
                ]
            )
            slope = [value * (1.0 - value) * share for value in colour]
            kept.append(
                (colour, share, through * left, slope, jax.nn.sigmoid(raw[0]) * spacing)
            )

        for part in range(parts):
            base = part * samples * 128
            own = slice(part * 128, (part + 1) * 128)
            colour, share, remain, slope, density_slope = kept[part]
            for copy in exchanges[part]:
                copy.wait()

            rank = [order_ref[step, r : r + 1, own] for r in range(regions)]
            depths = [gath_s[step, part, r, 0:1, :] for r in range(regions)]
            rendered = [jnp.zeros((1, 128), F32)] * 3
            lighted = []
            passing_own, rank_own = jnp.zeros((1, 128), F32), jnp.zeros((1, 128), jnp.int32)
            for r in range(regions):
                prior = jnp.zeros((1, 128), F32)
                for q in range(regions):
                    if q != r:
                        prior = prior + jnp.where(rank[q] < rank[r], depths[q], 0.0)
                passing = jnp.exp(-prior)
                lights = [passing * gath_s[step, part, r, c + 1 : c + 2, :] for c in range(3)]
                lighted.append(lights)
                rendered = [a + b for a, b in zip(rendered, lights)]
                passing_own = jnp.where(region == r, passing, passing_own)
                rank_own = jnp.where(region == r, rank[r], rank_own)
            error = [
                2.0 * (rendered[c] - targets_ref[c, step : step + 1, own]) / rays_total
                for c in range(3)
            ]
            d_depth = jnp.zeros((1, 128), F32)
            for r in range(regions):
                amount = sum(lighted[r][c] * error[c] for c in range(3))
                d_depth = d_depth - jnp.where(rank[r] > rank_own, amount, 0.0)
            d_colour = [passing_own * value for value in error]

            pull = sum(d_colour[c] * colour[c] for c in range(3))
            after = dot(later, pull * share, HIGH)
            d_optical = pull * remain - after + d_depth
            dout_s[part, pl.ds(0, samples, stride=16), :] = d_optical * density_slope
            for c in range(3):
                dout_s[part, pl.ds(c + 1, samples, stride=16), :] = d_colour[c] * slope[c]

            def backward(i, carry):
                here = pl.ds(pl.multiple_of(base + i * columns, columns), columns)
                d_out = jnp.concatenate(
                    [
                        dout_s[part, pl.ds(pl.multiple_of((i * SLOTS + s) * 16, 16), 16), :]
                        for s in range(SLOTS)
                    ],
                    1,
                ).astype(BF16)
                second = h2_s[:, here]
                first = h1_s[:, here]
                zero = jnp.zeros((), BF16)
                g3_s[...] += dot_nt(d_out, second)
                d_second = jnp.where(second > zero, dot(w3_s[...], d_out).astype(BF16), zero)
                d_first = jnp.where(first > zero, dot(w2_s[...], d_second).astype(BF16), zero)
                g2_s[...] += dot_nt(first, d_second)
                g1_s[...] += dot_nt(enc_s[step, :, here], d_first)
                return carry

            lax.fori_loop(0, chunks, backward, 0)

        for kind in range(2):
            for j in range(HALF):
                at = 8 * (kind * HALF + j)
                for side in range(2):
                    grad_s[
                        step, pl.ds(2 * (kind * 3 * FREQS + j) + side, 6, stride=FREQS), :
                    ] = g1_s[at : at + 6, side * 128 : (side + 1) * 128]
        for side in range(2):
            grad_s[step, pl.ds(FIRST + side, WIDTH, stride=2), :] = g2_s[
                :, side * 128 : (side + 1) * 128
            ]
        wide = jnp.concatenate(
            [jnp.broadcast_to(g3_s[c : c + 1, :], (8, WIDTH)) for c in range(4)], 1
        )
        wide = jnp.where(third_mask, wide, 0.0)
        high = wide.astype(BF16).astype(F32)
        middle = (wide - high).astype(BF16).astype(F32)
        low = wide - high - middle
        moved = dot(
            jnp.concatenate([high, middle, low, jnp.zeros_like(low)], 0).astype(BF16),
            third_s[...],
        )
        grad_s[step, SECOND : SECOND + 8, :] = moved[:8] + moved[8:16] + moved[16:24]

        inner = []
        for away in [*range(1, batches), 0]:
            at = lax.rem(batch + away, batches)
            inner.append(
                [
                    send(
                        grad_s.at[step, shard_rows(at, lax.rem(sub + offset, subs)), :],
                        core_s.at[step, away, offset - 1],
                        csend.at[step, away, offset - 1],
                        crecv.at[step, away, offset - 1],
                        sub_peer(offset),
                    )
                    for offset in range(1, subs)
                ]
            )
        outer = []
        for away, copies in zip([*range(1, batches), 0], inner):
            gradient = grad_s[step, shard_rows(lax.rem(batch + away, batches), sub), :]
            for offset, copy in enumerate(copies):
                copy.wait()
                gradient = gradient + core_s[step, away, offset]
            if away:
                chip_s[step, away - 1] = gradient
                outer.append(
                    send(
                        chip_s.at[step, away - 1],
                        part_s.at[step, away - 1],
                        rsend.at[step, away - 1],
                        rrecv.at[step, away - 1],
                        batch_peer(away),
                    )
                )
        if step + 1 < steps:
            for part in range(parts):
                encode(step + 1, part)
        for away, copy in enumerate(outer):
            copy.wait()
            gradient = gradient + part_s[step, away]
        mine = shard_rows(batch, sub)
        if step == 0:
            fetches[3].wait()
            fetches[4].wait()
            moment_one, moment_two = first_ref[0], second_ref[0]
            current = params_ref[0, mine, :]
        else:
            moment_one, moment_two = out_first[0], out_second[0]
            current = weights_s[step - 1, mine, :]
        moment_one = BETA_ONE * moment_one + (1.0 - BETA_ONE) * gradient
        moment_two = BETA_TWO * moment_two + (1.0 - BETA_TWO) * gradient * gradient
        weights_s[step, mine, :] = current - LEARNING_RATE * moment_one / (
            jnp.sqrt(moment_two) + ADAM_EPSILON
        )
        own = weights_s.at[step, mine, :]
        outer = [
            send(
                own, own, asend.at[step, away - 1], arecv.at[step, away - 1], batch_peer(away)
            )
            for away in range(1, batches)
        ]
        out_first[0] = moment_one
        out_second[0] = moment_two
        inner = []
        for away in range(batches):
            if away:
                outer[away - 1].wait()
            got = weights_s.at[step, shard_rows(lax.rem(batch + batches - away, batches), sub), :]
            inner += [
                send(
                    got,
                    got,
                    bsend.at[step, away, offset - 1],
                    brecv.at[step, away, offset - 1],
                    sub_peer(offset),
                )
                for offset in range(1, subs)
            ]
        for copy in inner:
            copy.wait()
    out_params[0] = weights_s[steps - 1]


def body(params, first_moment, second_moment, points, deltas, counts, order, targets):
    steps, _, _, samples, rays = points.shape
    regions = lax.axis_size("region")
    batches, subs = lax.axis_size("batch"), lax.axis_size("sub")
    total = samples * rays
    parts = rays // 128
    rows, lanes = params.shape[1:]
    shard = first_moment.shape[1]
    dma = pltpu.SemaphoreType.DMA
    vmem = pl.BlockSpec(memory_space=pltpu.VMEM)
    hbm = pl.BlockSpec(memory_space=pltpu.HBM)
    return pl.pallas_call(
        functools.partial(kernel, steps, regions, batches, subs),
        out_shape=(
            jax.ShapeDtypeStruct(params.shape, F32),
            jax.ShapeDtypeStruct(first_moment.shape, F32),
            jax.ShapeDtypeStruct(second_moment.shape, F32),
        ),
        in_specs=[hbm] * 5 + [vmem] * 3,
        out_specs=(vmem,) * 3,
        scratch_shapes=[
            *(
                pltpu.VMEM(x.shape, F32)
                for x in (params, first_moment, second_moment, points, deltas)
            ),
            pltpu.VMEM((steps, 16 * HALF, total), BF16),
            pltpu.VMEM((WIDTH, total), BF16),
            pltpu.VMEM((WIDTH, total), BF16),
            pltpu.VMEM((parts, samples * 8, 128), F32),
            pltpu.VMEM((parts, samples * 16, 128), F32),
            pltpu.VMEM((16 * HALF, WIDTH), F32),
            pltpu.VMEM((WIDTH, 16 * HALF), BF16),
            pltpu.VMEM((WIDTH, WIDTH), BF16),
            pltpu.VMEM((WIDTH, WIDTH), BF16),
            pltpu.VMEM((WIDTH, 16), BF16),
            pltpu.VMEM((16, WIDTH), BF16),
            pltpu.VMEM((4 * WIDTH, 128), BF16),
            pltpu.VMEM((16 * HALF, WIDTH), F32),
            pltpu.VMEM((WIDTH, WIDTH), F32),
            pltpu.VMEM((16, WIDTH), F32),
            pltpu.VMEM((steps, rows, lanes), F32),
            pltpu.VMEM((steps, rows, lanes), F32),
            pltpu.VMEM((steps, parts, regions, 8, 128), F32),
            pltpu.VMEM((steps, batches, subs - 1, shard, lanes), F32),
            pltpu.VMEM((steps, batches - 1, shard, lanes), F32),
            pltpu.VMEM((steps, batches - 1, shard, lanes), F32),
            dma((5,)),
            dma((steps, parts, regions - 1)),
            dma((steps, parts, regions - 1)),
            dma((steps, batches, subs - 1)),
            dma((steps, batches, subs - 1)),
            dma((steps, batches - 1)),
            dma((steps, batches - 1)),
            dma((steps, batches - 1)),
            dma((steps, batches - 1)),
            dma((steps, batches, subs - 1)),
            dma((steps, batches, subs - 1)),
        ],
        compiler_params=pltpu.CompilerParams(
            collective_id=0, has_side_effects=True, vmem_limit_bytes=48 * 1024 * 1024
        ),
    )(
        params,
        first_moment,
        second_moment,
        points,
        deltas,
        counts,
        jnp.transpose(order, (0, 2, 1)),
        jnp.transpose(targets, (1, 0, 2)),
    )


def solution(mesh):
    placed = (
        P(("grp", "region"), None, None),
        P(("grp", "region"), ("batch", "sub"), None),
        P(("grp", "region"), ("batch", "sub"), None),
        P(None, "region", None, None, ("grp", "batch", "sub")),
        P(None, "region", None, ("grp", "batch", "sub")),
        P(None, "region", ("grp", "batch", "sub")),
        P(None, ("grp", "batch", "sub"), None),
        P(None, None, ("grp", "batch", "sub")),
    )
    return jax.shard_map(
        body,
        mesh=mesh,
        in_specs=placed,
        out_specs=(
            P(("grp", "region"), None, None),
            P(("grp", "region"), ("batch", "sub"), None),
            P(("grp", "region"), ("batch", "sub"), None),
        ),
        check_vma=False,
    )
```

time: 64.3 us -> 55.7 us (0.87); the launches traced: 63.1 us -> 55.3 us
  Pallas kernels: 56.1 us -> 46 us
  local copies, waits for them, and re-layouts: 6.34 us -> 8.57 us
    pallas_call x1, Pallas kernels: 56.1 us -> 46 us  [body(): pl.pallas_call(functools.partial(kernel, steps, regions, batches, subs),...]
    unnamed x17 -> x19, local copies, waits for them, and re-layouts: 6.34 us -> 8.57 us
where the time goes in v2:
time: 55.7 us; the launch traced here: 55.3 us
  Pallas kernels  46 us (83%)
  local copies, waits for them, and re-layouts  8.57 us (15%)
  between operations  0.66 us (1%)
    pallas_call x1, Pallas kernels, body(): pl.pallas_call(functools.partial(kernel, steps, regions, batches, subs),...  46 us
    unnamed x19, local copies, waits for them, and re-layouts  8.57 us

profile of v2, /device:TPU:0, one launch (start us, length us, event | category | flops | bytes accessed | tf_op | source)
XLA Modules:
  0.0 55.3 jit_solution(10820864498530408411)
XLA Ops:
  0.6 0.0 copy-start.7
  0.6 0.7 %copy-done.7 = s32[2,1,256]{2,1,0:T(1,128)S(1)} copy-done((s32[2,1,256]{2,1,0:T(1,128)S(1)}, s32[2,1,256]{2,1,0:T(1,128)}, u32[]{:S(2)}) %copy-start.7) | copy-done | bytes 2072
  1.3 0.0 copy-start
  1.3 1.0 %copy-done = f32[1,640,128]{2,1,0:T(8,128)S(1)} copy-done((f32[1,640,128]{2,1,0:T(8,128)S(1)}, f32[1,640,128]{2,1,0:T(8,128)}, u32[]{:S(2)}) %copy-start) | copy-done | bytes 327704
  2.3 0.0 copy-start.1
  2.3 0.9 %copy-done.1 = f32[2,1,3,32,256]{4,3,2,1,0:T(8,128)S(1)} copy-done((f32[2,1,3,32,256]{4,3,2,1,0:T(8,128)S(1)}, f32[2,1,3,32,256]{4,3,2,1,0:T(8,128)}, u32[]{:S(2)}) %copy-start.1) | copy-done | bytes 196632
  3.2 0.0 copy-start.2
  3.2 0.9 %copy-done.2 = f32[1,160,128]{2,1,0:T(8,128)S(1)} copy-done((f32[1,160,128]{2,1,0:T(8,128)S(1)}, f32[1,160,128]{2,1,0:T(8,128)}, u32[]{:S(2)}) %copy-start.2) | copy-done | bytes 81944
  4.1 0.0 copy-start.3
  4.1 0.9 %copy-done.3 = f32[1,160,128]{2,1,0:T(8,128)S(1)} copy-done((f32[1,160,128]{2,1,0:T(8,128)S(1)}, f32[1,160,128]{2,1,0:T(8,128)}, u32[]{:S(2)}) %copy-start.3) | copy-done | bytes 81944
  5.0 0.0 copy-start.4
  5.0 0.8 %copy-done.4 = f32[2,1,32,256]{3,2,1,0:T(8,128)S(1)} copy-done((f32[2,1,32,256]{3,2,1,0:T(8,128)S(1)}, f32[2,1,32,256]{3,2,1,0:T(8,128)}, u32[]{:S(2)}) %copy-start.4) | copy-done | bytes 65560
  5.8 0.0 copy-start.5
  5.8 0.7 %copy-done.5 = s32[2,256,4]{1,2,0:T(4,128)S(1)} copy-done((s32[2,256,4]{1,2,0:T(4,128)S(1)}, s32[2,256,4]{1,2,0:T(4,128)}, u32[]{:S(2)}) %copy-start.5) | copy-done | bytes 8216
  6.5 0.0 copy-start.6
  6.5 0.7 %copy-done.6 = f32[2,3,256]{2,0,1:T(2,128)S(1)} copy-done((f32[2,3,256]{2,0,1:T(2,128)S(1)}, f32[2,3,256]{2,0,1:T(2,128)}, u32[]{:S(2)}) %copy-start.6) | copy-done | bytes 6168
  7.2 46.0 %shard_map.103 = (f32[1,640,128]{2,1,0:T(8,128)S(1)}, f32[1,160,128]{2,1,0:T(8,128)S(1)}, f32[1,160,128]{2,1,0:T(8,128)S(1)}) custom-call(f32[1,640,128]{2,1,0:T(8,128)S(1)} %copy-done, f32[1,160,128]{2,1,0:T(8,128)S(1)} %copy-done.2, f32[1,160,128]{2,1,0:T(8,128)S(1)} %copy-done.3, f32[2,1,3,32,256]{4,3,2,1,0:T(8,128)S(1)} %copy-done.1, ...), custom_call_target="tpu_custom_call" | custom-call | tf_op jit(solution)/shard_map/pallas_call | solution.py:504
  53.3 0.7 %copy.14 = f32[1,640,128]{2,1,0:T(8,128)} copy(f32[1,640,128]{2,1,0:T(8,128)S(1)} %get-tuple-element.6) | data formatting | bytes 655360
  54.0 0.6 %copy.15 = f32[1,160,128]{2,1,0:T(8,128)} copy(f32[1,160,128]{2,1,0:T(8,128)S(1)} %get-tuple-element.7) | data formatting | bytes 163840
  54.6 0.6 %copy.16 = f32[1,160,128]{2,1,0:T(8,128)} copy(f32[1,160,128]{2,1,0:T(8,128)S(1)} %get-tuple-element.8) | data formatting | bytes 163840
Async XLA Ops:
  0.6 0.7 %copy-start.7 = (s32[2,1,256]{2,1,0:T(1,128)S(1)}, s32[2,1,256]{2,1,0:T(1,128)}, u32[]{:S(2)}) copy-start(s32[2,1,256]{2,1,0:T(1,128)} %counts_ref.1) | copy-start | bytes 6148
  1.3 1.0 %copy-start = (f32[1,640,128]{2,1,0:T(8,128)S(1)}, f32[1,640,128]{2,1,0:T(8,128)}, u32[]{:S(2)}) copy-start(f32[1,640,128]{2,1,0:T(8,128)} %params_hbm.1) | copy-start | bytes 983044
  2.3 0.9 %copy-start.1 = (f32[2,1,3,32,256]{4,3,2,1,0:T(8,128)S(1)}, f32[2,1,3,32,256]{4,3,2,1,0:T(8,128)}, u32[]{:S(2)}) copy-start(f32[2,1,3,32,256]{4,3,2,1,0:T(8,128)} %points_hbm.1) | copy-start | bytes 589828
  3.2 0.9 %copy-start.2 = (f32[1,160,128]{2,1,0:T(8,128)S(1)}, f32[1,160,128]{2,1,0:T(8,128)}, u32[]{:S(2)}) copy-start(f32[1,160,128]{2,1,0:T(8,128)} %first_hbm.1) | copy-start | bytes 245764
  4.1 0.9 %copy-start.3 = (f32[1,160,128]{2,1,0:T(8,128)S(1)}, f32[1,160,128]{2,1,0:T(8,128)}, u32[]{:S(2)}) copy-start(f32[1,160,128]{2,1,0:T(8,128)} %second_hbm.1) | copy-start | bytes 245764
  5.0 0.8 %copy-start.4 = (f32[2,1,32,256]{3,2,1,0:T(8,128)S(1)}, f32[2,1,32,256]{3,2,1,0:T(8,128)}, u32[]{:S(2)}) copy-start(f32[2,1,32,256]{3,2,1,0:T(8,128)} %deltas_hbm.1) | copy-start | bytes 196612
  5.8 0.7 %copy-start.5 = (s32[2,256,4]{1,2,0:T(4,128)S(1)}, s32[2,256,4]{1,2,0:T(4,128)}, u32[]{:S(2)}) copy-start(s32[2,256,4]{1,2,0:T(4,128)} %param.14) | copy-start | bytes 24580
  6.5 0.7 %copy-start.6 = (f32[2,3,256]{2,0,1:T(2,128)S(1)}, f32[2,3,256]{2,0,1:T(2,128)}, u32[]{:S(2)}) copy-start(f32[2,3,256]{2,0,1:T(2,128)} %param.15) | copy-start | bytes 18436

commit v3 on v2

--- a/solution.py
+++ b/solution.py
@@ -36,6 +36,17 @@
     return lax.dot_general(
         a, b, (((1,), (1,)), ((), ())), precision=precision, preferred_element_type=F32
     )
+
+
+def aligned(index, multiple):
+    return index if isinstance(index, int) else pl.multiple_of(index, multiple)
+
+
+def repeat(count, step):
+    if count == 1:
+        step(0, 0)
+    else:
+        lax.fori_loop(0, count, step, 0)
 
 
 def iota(shape, dim):
@@ -161,7 +172,7 @@
         return {"sub": lax.rem(sub + offset, subs)}
 
     def shard_rows(batch_at, sub_at):
-        return pl.ds(pl.multiple_of((batch_at * subs + sub_at) * shard, 8), shard)
+        return pl.ds(aligned((batch_at * subs + sub_at) * shard, 8), shard)
 
     def send(source, target, send_sem, recv_sem, where):
         copy = pltpu.make_async_remote_copy(
@@ -203,7 +214,7 @@
                     step,
                     0,
                     c,
-                    pl.ds(pl.multiple_of(i * SLOTS, SLOTS), SLOTS),
+                    pl.ds(aligned(i * SLOTS, SLOTS), SLOTS),
                     part * 128 : (part + 1) * 128,
                 ]
                 for c in range(3)
@@ -220,18 +231,18 @@
                     sine, cosine = doubled(sine, cosine)
                     sines.append(sine)
                     cosines.append(cosine)
-                at = pl.multiple_of(part * samples * 128 + t * 128, 128)
+                at = aligned(part * samples * 128 + t * 128, 128)
                 enc_s[step, :, pl.ds(at, 128)] = jnp.concatenate(sines + cosines, 0).astype(
                     BF16
                 )
             return carry
 
-        lax.fori_loop(0, chunks, chunk, 0)
+        repeat(chunks, chunk)
 
     fetches[0].wait()
+    fetches[1].wait()
     for part in range(parts):
         encode(0, part)
-    fetches[1].wait()
 
     for step in range(steps):
 
@@ -271,19 +282,19 @@
             own = slice(part * 128, (part + 1) * 128)
 
             def forward(i, carry):
-                here = pl.ds(pl.multiple_of(base + i * columns, columns), columns)
+                here = pl.ds(aligned(base + i * columns, columns), columns)
                 first = jnp.maximum(dot(w1t_s[...], enc_s[step, :, here]), 0.0).astype(BF16)
                 h1_s[:, here] = first
                 second = jnp.maximum(dot(w2t_s[...], first), 0.0).astype(BF16)
                 h2_s[:, here] = second
                 out = dot(w3t_s[...], second)
                 for s in range(SLOTS):
-                    raw_s[part, pl.ds(pl.multiple_of((i * SLOTS + s) * 8, 8), 8), :] = out[
+                    raw_s[part, pl.ds(aligned((i * SLOTS + s) * 8, 8), 8), :] = out[
                         :8, s * 128 : (s + 1) * 128
                     ]
                 return carry
 
-            lax.fori_loop(0, chunks, forward, 0)
+            repeat(chunks, forward)
 
             if step == 0 and part == 0:
                 fetches[2].wait()
@@ -365,10 +376,10 @@
                 dout_s[part, pl.ds(c + 1, samples, stride=16), :] = d_colour[c] * slope[c]
 
             def backward(i, carry):
-                here = pl.ds(pl.multiple_of(base + i * columns, columns), columns)
+                here = pl.ds(aligned(base + i * columns, columns), columns)
                 d_out = jnp.concatenate(
                     [
-                        dout_s[part, pl.ds(pl.multiple_of((i * SLOTS + s) * 16, 16), 16), :]
+                        dout_s[part, pl.ds(aligned((i * SLOTS + s) * 16, 16), 16), :]
                         for s in range(SLOTS)
                     ],
                     1,
@@ -383,7 +394,7 @@
                 g1_s[...] += dot_nt(enc_s[step, :, here], d_first)
                 return carry
 
-            lax.fori_loop(0, chunks, backward, 0)
+            repeat(chunks, backward)
 
         for kind in range(2):
             for j in range(HALF):

time: 55.7 us -> 55.7 us (level)
  no operation moved by 1% of the time
where the time goes in v3:
time: 55.7 us; the launch traced here: 55.3 us
  Pallas kernels  46.1 us (83%)
  local copies, waits for them, and re-layouts  8.57 us (15%)
  between operations  0.66 us (1%)
    pallas_call x1, Pallas kernels, body(): pl.pallas_call(functools.partial(kernel, steps, regions, batches, subs),...  46.1 us
    unnamed x19, local copies, waits for them, and re-layouts  8.57 us

profile of v3, /device:TPU:0, one launch (start us, length us, event | category | flops | bytes accessed | tf_op | source)
XLA Modules:
  0.0 55.3 jit_solution(12323773233295620268)
XLA Ops:
  0.6 0.0 copy-start.7
  0.6 0.7 %copy-done.7 = s32[2,1,256]{2,1,0:T(1,128)S(1)} copy-done((s32[2,1,256]{2,1,0:T(1,128)S(1)}, s32[2,1,256]{2,1,0:T(1,128)}, u32[]{:S(2)}) %copy-start.7) | copy-done | bytes 2072
  1.3 0.0 copy-start
  1.3 1.0 %copy-done = f32[1,640,128]{2,1,0:T(8,128)S(1)} copy-done((f32[1,640,128]{2,1,0:T(8,128)S(1)}, f32[1,640,128]{2,1,0:T(8,128)}, u32[]{:S(2)}) %copy-start) | copy-done | bytes 327704
  2.3 0.0 copy-start.1
  2.3 0.9 %copy-done.1 = f32[2,1,3,32,256]{4,3,2,1,0:T(8,128)S(1)} copy-done((f32[2,1,3,32,256]{4,3,2,1,0:T(8,128)S(1)}, f32[2,1,3,32,256]{4,3,2,1,0:T(8,128)}, u32[]{:S(2)}) %copy-start.1) | copy-done | bytes 196632
  3.2 0.0 copy-start.2
  3.2 0.9 %copy-done.2 = f32[1,160,128]{2,1,0:T(8,128)S(1)} copy-done((f32[1,160,128]{2,1,0:T(8,128)S(1)}, f32[1,160,128]{2,1,0:T(8,128)}, u32[]{:S(2)}) %copy-start.2) | copy-done | bytes 81944
  4.1 0.0 copy-start.3
  4.1 0.9 %copy-done.3 = f32[1,160,128]{2,1,0:T(8,128)S(1)} copy-done((f32[1,160,128]{2,1,0:T(8,128)S(1)}, f32[1,160,128]{2,1,0:T(8,128)}, u32[]{:S(2)}) %copy-start.3) | copy-done | bytes 81944
  5.0 0.0 copy-start.4
  5.0 0.8 %copy-done.4 = f32[2,1,32,256]{3,2,1,0:T(8,128)S(1)} copy-done((f32[2,1,32,256]{3,2,1,0:T(8,128)S(1)}, f32[2,1,32,256]{3,2,1,0:T(8,128)}, u32[]{:S(2)}) %copy-start.4) | copy-done | bytes 65560
  5.8 0.0 copy-start.5
  5.8 0.7 %copy-done.5 = s32[2,256,4]{1,2,0:T(4,128)S(1)} copy-done((s32[2,256,4]{1,2,0:T(4,128)S(1)}, s32[2,256,4]{1,2,0:T(4,128)}, u32[]{:S(2)}) %copy-start.5) | copy-done | bytes 8216
  6.5 0.0 copy-start.6
  6.5 0.7 %copy-done.6 = f32[2,3,256]{2,0,1:T(2,128)S(1)} copy-done((f32[2,3,256]{2,0,1:T(2,128)S(1)}, f32[2,3,256]{2,0,1:T(2,128)}, u32[]{:S(2)}) %copy-start.6) | copy-done | bytes 6168
  7.2 46.1 %shard_map.103 = (f32[1,640,128]{2,1,0:T(8,128)S(1)}, f32[1,160,128]{2,1,0:T(8,128)S(1)}, f32[1,160,128]{2,1,0:T(8,128)S(1)}) custom-call(f32[1,640,128]{2,1,0:T(8,128)S(1)} %copy-done, f32[1,160,128]{2,1,0:T(8,128)S(1)} %copy-done.2, f32[1,160,128]{2,1,0:T(8,128)S(1)} %copy-done.3, f32[2,1,3,32,256]{4,3,2,1,0:T(8,128)S(1)} %copy-done.1, ...), custom_call_target="tpu_custom_call" | custom-call | tf_op jit(solution)/shard_map/pallas_call | solution.py:515
  53.3 0.7 %copy.14 = f32[1,640,128]{2,1,0:T(8,128)} copy(f32[1,640,128]{2,1,0:T(8,128)S(1)} %get-tuple-element.6) | data formatting | bytes 655360
  54.0 0.6 %copy.15 = f32[1,160,128]{2,1,0:T(8,128)} copy(f32[1,160,128]{2,1,0:T(8,128)S(1)} %get-tuple-element.7) | data formatting | bytes 163840
  54.6 0.6 %copy.16 = f32[1,160,128]{2,1,0:T(8,128)} copy(f32[1,160,128]{2,1,0:T(8,128)S(1)} %get-tuple-element.8) | data formatting | bytes 163840
Async XLA Ops:
  0.6 0.7 %copy-start.7 = (s32[2,1,256]{2,1,0:T(1,128)S(1)}, s32[2,1,256]{2,1,0:T(1,128)}, u32[]{:S(2)}) copy-start(s32[2,1,256]{2,1,0:T(1,128)} %counts_ref.1) | copy-start | bytes 6148
  1.3 1.0 %copy-start = (f32[1,640,128]{2,1,0:T(8,128)S(1)}, f32[1,640,128]{2,1,0:T(8,128)}, u32[]{:S(2)}) copy-start(f32[1,640,128]{2,1,0:T(8,128)} %params_hbm.1) | copy-start | bytes 983044
  2.3 0.9 %copy-start.1 = (f32[2,1,3,32,256]{4,3,2,1,0:T(8,128)S(1)}, f32[2,1,3,32,256]{4,3,2,1,0:T(8,128)}, u32[]{:S(2)}) copy-start(f32[2,1,3,32,256]{4,3,2,1,0:T(8,128)} %points_hbm.1) | copy-start | bytes 589828
  3.2 0.9 %copy-start.2 = (f32[1,160,128]{2,1,0:T(8,128)S(1)}, f32[1,160,128]{2,1,0:T(8,128)}, u32[]{:S(2)}) copy-start(f32[1,160,128]{2,1,0:T(8,128)} %first_hbm.1) | copy-start | bytes 245764
  4.1 0.9 %copy-start.3 = (f32[1,160,128]{2,1,0:T(8,128)S(1)}, f32[1,160,128]{2,1,0:T(8,128)}, u32[]{:S(2)}) copy-start(f32[1,160,128]{2,1,0:T(8,128)} %second_hbm.1) | copy-start | bytes 245764
  5.0 0.8 %copy-start.4 = (f32[2,1,32,256]{3,2,1,0:T(8,128)S(1)}, f32[2,1,32,256]{3,2,1,0:T(8,128)}, u32[]{:S(2)}) copy-start(f32[2,1,32,256]{3,2,1,0:T(8,128)} %deltas_hbm.1) | copy-start | bytes 196612
  5.8 0.7 %copy-start.5 = (s32[2,256,4]{1,2,0:T(4,128)S(1)}, s32[2,256,4]{1,2,0:T(4,128)}, u32[]{:S(2)}) copy-start(s32[2,256,4]{1,2,0:T(4,128)} %param.14) | copy-start | bytes 24580
  6.5 0.7 %copy-start.6 = (f32[2,3,256]{2,0,1:T(2,128)S(1)}, f32[2,3,256]{2,0,1:T(2,128)}, u32[]{:S(2)}) copy-start(f32[2,3,256]{2,0,1:T(2,128)} %param.15) | copy-start | bytes 18436
